TPU v7x, 32 devices: a whole 2x2x4 slice. The times are simulated.
32 devices in a mesh: row: 2 (over core), col: 4 (over y, x), layer: 4 (over z).
Axes of the slice: x: 2, y: 2, z: 4, core: 2. Of those that a mesh axis runs over, the one named last changes fastest.
Arguments:
- left_mant: bfloat16 [3, 5, 6, 1024, 4, 256], P(None, None, None, ('row', 'col'), 'layer'), may hold values from 9.983778e-07 to 1
- right_mant: bfloat16 [3, 5, 6, 4, 256, 1024], P(None, None, None, 'layer', 'row', 'col'), may hold values from 9.983778e-07 to 1
- left_scale: float32 [3, 5], replicated, may hold values from -750 to 0
- right_scale: float32 [3, 5], replicated, may hold values from -750 to 0
- rule_probs: float32 [6, 6, 6], replicated, may hold values from 0.05 to 1
- pair_logp: float32 [6, 4, 4], replicated, may hold values from -4 to 4
- nucleotides: int32 [65536], replicated, may hold values from 0 to 3
- first_block: int32 [1], replicated, may hold values from 0 to 55
Outputs:
- block_values: float32 [3, 6, 1024, 1024], P(None, None, ('row', 'layer'), 'col')
- block_scale: float32 [3], replicated
All inputs are finite; a program needn't handle non-finite values.
Results may differ from a plain program's by a relative error of at most 0.0003.
Values may be sent and summed in bfloat16 or wider, within the bound.
A program may use at most 128 MiB of HBM per device.

v0:
```python
from functools import partial

import jax
import jax.numpy as jnp
from jax import lax
from jax.sharding import PartitionSpec as P


def add_pieces(left_full, mix_block, running, arrived, anchor):
    channels = arrived.shape[1]

    def one_split(split_id, partial_sum):
        left_part = lax.dynamic_index_in_dim(left_full, split_id, 0, False)
        mixing_now = lax.dynamic_index_in_dim(mix_block, split_id, 0, False)
        mixed_part = jnp.einsum(
            "xyz,yiqn->xziqn", mixing_now, left_part, preferred_element_type=jnp.float32
        ).astype(jnp.bfloat16)
        mixed_part = mixed_part.reshape(channels, channels, left_part.shape[1], -1)
        right_part = lax.dynamic_index_in_dim(arrived, split_id, 0, False)
        right_part = right_part.reshape(channels, -1, right_part.shape[3])
        return partial_sum + jnp.einsum(
            "xzik,zkj->xij", mixed_part, right_part, preferred_element_type=jnp.float32
        )

    return lax.fori_loop(0, arrived.shape[0], one_split, running)


def take_codes(nucleotides, length, position):
    return lax.dynamic_slice_in_dim(nucleotides, position, length)


def local(
    left_mant, right_mant, left_scale, right_scale, rule_probs, pair_logp, nucleotides, first_block
):
    total_scale = left_scale + right_scale
    highest = jnp.max(total_scale, axis=1)
    weight = jnp.exp(total_scale - highest[:, None])
    mixing = (rule_probs[None, None] * weight[:, :, None, None, None]).astype(jnp.bfloat16)
    count_out = left_mant.shape[0]
    count_split = left_mant.shape[1]
    channels = left_mant.shape[2]
    layers = lax.axis_size("layer")
    partials = []
    for block_id in range(count_out):
        left_rows_all = lax.all_gather(left_mant[block_id], "col", axis=2, tiled=True)
        right_ready = right_mant[block_id]
        accumulate = partial(add_pieces, left_rows_all, mixing[block_id])
        zeroed = jnp.zeros((channels, left_rows_all.shape[2], right_ready.shape[4]), jnp.float32)
        partials.append(
            accumulate(zeroed, lax.all_gather(right_ready, "row", axis=3, tiled=True), jnp.int32(0))
        )
    summed = jnp.stack(partials)
    summed = lax.psum_scatter(summed, "layer", scatter_dimension=2, tiled=True)
    rows_final = summed.shape[2]
    cols_final = summed.shape[3]
    block_len = cols_final * lax.axis_size("col")
    row_anchor = (lax.axis_index("row") * layers + lax.axis_index("layer")) * rows_final
    col_anchor = lax.axis_index("col") * cols_final
    offsets = jnp.arange(count_out, dtype=jnp.int32) + first_block[0]
    row_codes = jax.vmap(partial(take_codes, nucleotides, rows_final))(
        offsets * block_len + row_anchor
    )
    col_codes = jax.vmap(partial(take_codes, nucleotides, cols_final))(
        (offsets + count_split + 1) * block_len + col_anchor
    )
    symbols = jnp.arange(4, dtype=jnp.int32)
    row_hot = (row_codes[:, :, None] == symbols).astype(jnp.float32)
    col_hot = (col_codes[:, :, None] == symbols).astype(jnp.float32)
    pairing = jnp.einsum(
        "biu,xuv,bjv->bxij", row_hot, pair_logp, col_hot, precision=lax.Precision.HIGHEST
    )
    inside = highest[:, None, None, None] + jnp.log(summed) + pairing
    peak_value = lax.pmax(jnp.max(inside, axis=(1, 2, 3)), ("row", "col", "layer"))
    return (inside - peak_value[:, None, None, None], peak_value)


def solution(mesh):
    in_specs = (
        P(None, None, None, ("row", "col"), "layer", None),
        P(None, None, None, "layer", "row", "col"),
        P(),
        P(),
        P(),
        P(),
        P(),
        P(),
    )
    out_specs = (P(None, None, ("row", "layer"), "col"), P())
    return jax.shard_map(local, mesh=mesh, in_specs=in_specs, out_specs=out_specs, check_vma=False)
```

profile of v0, /device:TPU:0, one launch (start us, length us, event | category | flops | bytes accessed | tf_op | source)
XLA Modules:
  0.0 651.3 jit_solution(289785120327765519)
XLA Ops:
  28.8 86.3 %all-gather.17.cloned.1.call-done = bf16[1,5,6,512,1,256]{5,3,2,1,4,0:T(8,128)(2,1)} async-done(((bf16[1,5,6,128,1,256]{5,3,2,1,4,0:T(8,128)(2,1)}), bf16[1,5,6,512,1,256]{5,3,2,1,4,0:T(8,128)(2,1)}) %all-gather.17.cloned.1.call-update) | async-done | bytes 7864336 | tf_op jit(solution)/shard_map/all_gather | solution.py:45
  115.1 108.5 %while.47 = (s32[]{:T(128)}, f32[6,512,256]{2,1,0:T(8,128)}, bf16[5,6,6,6]{3,2,1,0:T(8,128)(2,1)S(1)}, bf16[5,6,512,1,256]{4,2,1,3,0:T(8,128)(2,1)}, bf16[5,6,1,...) while((s32[]{:T(128)}, f32[6,512,256]{2,1,0:T(8,128)}, bf16[5,6,6,6]{3,2,1,0:T(8,128)(2,1)S(1)}, ...), condition=%wide.region_4.5_spmd.clone, body=%wide.region_3.4_spmd.clone.sunk | while | flops 2474115072 | bytes 33829468 | solution.py:25
  116.7 8.8 %fusion.58 = bf16[6,6,512,256]{3,1,2,0:T(8,128)(2,1)} fusion(bf16[6,512,256,1]{2,1,0,3:T(8,128)(2,1)S(1)} %dynamic-slice_bitcast_fusion.10, bf16[5,6,6,6]{3,2,1,0:T(8,128)(2,1)S(1)} %get-tuple-element.649, s32[]{:T(128)} %get-tuple-element.640), kind=kOutput, calls=%fused_computation.18.clone.1 | convolution fusion | flops 56623104 | bytes 11022340 | tf_op jit(solution)/shard_map/while/body/eval_jaxpr/xyz,yiqn->xziqn/dot_general | solution.py:15
  125.4 11.0 %bitcast_add_fusion.7 = f32[6,512,256]{2,1,0:T(8,128)} fusion(f32[6,512,256]{2,1,0:T(8,128)} %get-tuple-element.641, bf16[6,6,512,256]{3,1,2,0:T(8,128)(2,1)} %fusion.58, pred[]{:T(512)S(6)} %compare.14, bf16[5,6,1,256,256]{4,3,1,2,0:T(8,128)(2,1)} %get-tuple-element.651, s32[]{:T(128)} %get-tuple-element.640), kind=kOutput, calls=%fused_computation.17.clone.1 | convolution fusion | flops 2417491968 | bytes 19661312 | tf_op jit(solution)/shard_map/while/body/eval_jaxpr/xzik,zkj->xij/dot_general | solution.py:21
  137.9 8.8 %fusion.58 = bf16[6,6,512,256]{3,1,2,0:T(8,128)(2,1)} fusion(bf16[6,512,256,1]{2,1,0,3:T(8,128)(2,1)S(1)} %dynamic-slice_bitcast_fusion.10, bf16[5,6,6,6]{3,2,1,0:T(8,128)(2,1)S(1)} %get-tuple-element.649, s32[]{:T(128)} %get-tuple-element.640), kind=kOutput, calls=%fused_computation.18.clone.1 | convolution fusion | flops 56623104 | bytes 11022340 | tf_op jit(solution)/shard_map/while/body/eval_jaxpr/xyz,yiqn->xziqn/dot_general | solution.py:15
  146.7 11.2 %bitcast_add_fusion.7 = f32[6,512,256]{2,1,0:T(8,128)} fusion(f32[6,512,256]{2,1,0:T(8,128)} %get-tuple-element.641, bf16[6,6,512,256]{3,1,2,0:T(8,128)(2,1)} %fusion.58, pred[]{:T(512)S(6)} %compare.14, bf16[5,6,1,256,256]{4,3,1,2,0:T(8,128)(2,1)} %get-tuple-element.651, s32[]{:T(128)} %get-tuple-element.640), kind=kOutput, calls=%fused_computation.17.clone.1 | convolution fusion | flops 2417491968 | bytes 19661312 | tf_op jit(solution)/shard_map/while/body/eval_jaxpr/xzik,zkj->xij/dot_general | solution.py:21
  159.4 8.8 %fusion.58 = bf16[6,6,512,256]{3,1,2,0:T(8,128)(2,1)} fusion(bf16[6,512,256,1]{2,1,0,3:T(8,128)(2,1)S(1)} %dynamic-slice_bitcast_fusion.10, bf16[5,6,6,6]{3,2,1,0:T(8,128)(2,1)S(1)} %get-tuple-element.649, s32[]{:T(128)} %get-tuple-element.640), kind=kOutput, calls=%fused_computation.18.clone.1 | convolution fusion | flops 56623104 | bytes 11022340 | tf_op jit(solution)/shard_map/while/body/eval_jaxpr/xyz,yiqn->xziqn/dot_general | solution.py:15
  168.2 12.5 %bitcast_add_fusion.7 = f32[6,512,256]{2,1,0:T(8,128)} fusion(f32[6,512,256]{2,1,0:T(8,128)} %get-tuple-element.641, bf16[6,6,512,256]{3,1,2,0:T(8,128)(2,1)} %fusion.58, pred[]{:T(512)S(6)} %compare.14, bf16[5,6,1,256,256]{4,3,1,2,0:T(8,128)(2,1)} %get-tuple-element.651, s32[]{:T(128)} %get-tuple-element.640), kind=kOutput, calls=%fused_computation.17.clone.1 | convolution fusion | flops 2417491968 | bytes 19661312 | tf_op jit(solution)/shard_map/while/body/eval_jaxpr/xzik,zkj->xij/dot_general | solution.py:21
  191.0 11.2 %bitcast_add_fusion.7 = f32[6,512,256]{2,1,0:T(8,128)} fusion(f32[6,512,256]{2,1,0:T(8,128)} %get-tuple-element.641, bf16[6,6,512,256]{3,1,2,0:T(8,128)(2,1)} %fusion.58, pred[]{:T(512)S(6)} %compare.14, bf16[5,6,1,256,256]{4,3,1,2,0:T(8,128)(2,1)} %get-tuple-element.651, s32[]{:T(128)} %get-tuple-element.640), kind=kOutput, calls=%fused_computation.17.clone.1 | convolution fusion | flops 2417491968 | bytes 19661312 | tf_op jit(solution)/shard_map/while/body/eval_jaxpr/xzik,zkj->xij/dot_general | solution.py:21
  203.7 8.8 %fusion.58 = bf16[6,6,512,256]{3,1,2,0:T(8,128)(2,1)} fusion(bf16[6,512,256,1]{2,1,0,3:T(8,128)(2,1)S(1)} %dynamic-slice_bitcast_fusion.10, bf16[5,6,6,6]{3,2,1,0:T(8,128)(2,1)S(1)} %get-tuple-element.649, s32[]{:T(128)} %get-tuple-element.640), kind=kOutput, calls=%fused_computation.18.clone.1 | convolution fusion | flops 56623104 | bytes 11022340 | tf_op jit(solution)/shard_map/while/body/eval_jaxpr/xyz,yiqn->xziqn/dot_general | solution.py:15
  212.5 11.2 %bitcast_add_fusion.7 = f32[6,512,256]{2,1,0:T(8,128)} fusion(f32[6,512,256]{2,1,0:T(8,128)} %get-tuple-element.641, bf16[6,6,512,256]{3,1,2,0:T(8,128)(2,1)} %fusion.58, pred[]{:T(512)S(6)} %compare.14, bf16[5,6,1,256,256]{4,3,1,2,0:T(8,128)(2,1)} %get-tuple-element.651, s32[]{:T(128)} %get-tuple-element.640), kind=kOutput, calls=%fused_computation.17.clone.1 | convolution fusion | flops 2417491968 | bytes 19661312 | tf_op jit(solution)/shard_map/while/body/eval_jaxpr/xzik,zkj->xij/dot_general | solution.py:21
  223.7 106.3 %while.48 = (s32[]{:T(128)}, f32[6,512,256]{2,1,0:T(8,128)}, bf16[5,6,6,6]{3,2,1,0:T(8,128)(2,1)S(1)}, bf16[5,6,512,1,256]{4,2,1,3,0:T(8,128)(2,1)}, bf16[5,6,1,...) while((s32[]{:T(128)}, f32[6,512,256]{2,1,0:T(8,128)}, bf16[5,6,6,6]{3,2,1,0:T(8,128)(2,1)S(1)}, ...), condition=%wide.region_6.7_spmd.clone, body=%wide.region_5.6_spmd.clone.sunk | while | flops 2474115072 | bytes 33829468 | solution.py:25
  225.4 8.8 %fusion.62 = bf16[6,6,512,256]{3,1,2,0:T(8,128)(2,1)} fusion(bf16[6,512,256,1]{2,1,0,3:T(8,128)(2,1)S(1)} %dynamic-slice_bitcast_fusion.11, bf16[5,6,6,6]{3,2,1,0:T(8,128)(2,1)S(1)} %get-tuple-element.628, s32[]{:T(128)} %get-tuple-element.619), kind=kOutput, calls=%fused_computation.30.clone.1 | convolution fusion | flops 56623104 | bytes 11022340 | tf_op jit(solution)/shard_map/while/body/eval_jaxpr/xyz,yiqn->xziqn/dot_general | solution.py:15
  234.2 10.1 %bitcast_add_fusion.8 = f32[6,512,256]{2,1,0:T(8,128)} fusion(f32[6,512,256]{2,1,0:T(8,128)} %get-tuple-element.620, bf16[6,6,512,256]{3,1,2,0:T(8,128)(2,1)} %fusion.62, pred[]{:T(512)S(6)} %compare.15, bf16[5,6,1,256,256]{4,3,1,2,0:T(8,128)(2,1)} %get-tuple-element.630, s32[]{:T(128)} %get-tuple-element.619), kind=kOutput, calls=%fused_computation.29.clone.1 | convolution fusion | flops 2417491968 | bytes 19661312 | tf_op jit(solution)/shard_map/while/body/eval_jaxpr/xzik,zkj->xij/dot_general | solution.py:21
  246.1 8.8 %fusion.62 = bf16[6,6,512,256]{3,1,2,0:T(8,128)(2,1)} fusion(bf16[6,512,256,1]{2,1,0,3:T(8,128)(2,1)S(1)} %dynamic-slice_bitcast_fusion.11, bf16[5,6,6,6]{3,2,1,0:T(8,128)(2,1)S(1)} %get-tuple-element.628, s32[]{:T(128)} %get-tuple-element.619), kind=kOutput, calls=%fused_computation.30.clone.1 | convolution fusion | flops 56623104 | bytes 11022340 | tf_op jit(solution)/shard_map/while/body/eval_jaxpr/xyz,yiqn->xziqn/dot_general | solution.py:15
  254.9 11.1 %bitcast_add_fusion.8 = f32[6,512,256]{2,1,0:T(8,128)} fusion(f32[6,512,256]{2,1,0:T(8,128)} %get-tuple-element.620, bf16[6,6,512,256]{3,1,2,0:T(8,128)(2,1)} %fusion.62, pred[]{:T(512)S(6)} %compare.15, bf16[5,6,1,256,256]{4,3,1,2,0:T(8,128)(2,1)} %get-tuple-element.630, s32[]{:T(128)} %get-tuple-element.619), kind=kOutput, calls=%fused_computation.29.clone.1 | convolution fusion | flops 2417491968 | bytes 19661312 | tf_op jit(solution)/shard_map/while/body/eval_jaxpr/xzik,zkj->xij/dot_general | solution.py:21
  276.2 11.1 %bitcast_add_fusion.8 = f32[6,512,256]{2,1,0:T(8,128)} fusion(f32[6,512,256]{2,1,0:T(8,128)} %get-tuple-element.620, bf16[6,6,512,256]{3,1,2,0:T(8,128)(2,1)} %fusion.62, pred[]{:T(512)S(6)} %compare.15, bf16[5,6,1,256,256]{4,3,1,2,0:T(8,128)(2,1)} %get-tuple-element.630, s32[]{:T(128)} %get-tuple-element.619), kind=kOutput, calls=%fused_computation.29.clone.1 | convolution fusion | flops 2417491968 | bytes 19661312 | tf_op jit(solution)/shard_map/while/body/eval_jaxpr/xzik,zkj->xij/dot_general | solution.py:21
  288.8 8.8 %fusion.62 = bf16[6,6,512,256]{3,1,2,0:T(8,128)(2,1)} fusion(bf16[6,512,256,1]{2,1,0,3:T(8,128)(2,1)S(1)} %dynamic-slice_bitcast_fusion.11, bf16[5,6,6,6]{3,2,1,0:T(8,128)(2,1)S(1)} %get-tuple-element.628, s32[]{:T(128)} %get-tuple-element.619), kind=kOutput, calls=%fused_computation.30.clone.1 | convolution fusion | flops 56623104 | bytes 11022340 | tf_op jit(solution)/shard_map/while/body/eval_jaxpr/xyz,yiqn->xziqn/dot_general | solution.py:15
  297.6 11.1 %bitcast_add_fusion.8 = f32[6,512,256]{2,1,0:T(8,128)} fusion(f32[6,512,256]{2,1,0:T(8,128)} %get-tuple-element.620, bf16[6,6,512,256]{3,1,2,0:T(8,128)(2,1)} %fusion.62, pred[]{:T(512)S(6)} %compare.15, bf16[5,6,1,256,256]{4,3,1,2,0:T(8,128)(2,1)} %get-tuple-element.630, s32[]{:T(128)} %get-tuple-element.619), kind=kOutput, calls=%fused_computation.29.clone.1 | convolution fusion | flops 2417491968 | bytes 19661312 | tf_op jit(solution)/shard_map/while/body/eval_jaxpr/xzik,zkj->xij/dot_general | solution.py:21
  318.9 11.1 %bitcast_add_fusion.8 = f32[6,512,256]{2,1,0:T(8,128)} fusion(f32[6,512,256]{2,1,0:T(8,128)} %get-tuple-element.620, bf16[6,6,512,256]{3,1,2,0:T(8,128)(2,1)} %fusion.62, pred[]{:T(512)S(6)} %compare.15, bf16[5,6,1,256,256]{4,3,1,2,0:T(8,128)(2,1)} %get-tuple-element.630, s32[]{:T(128)} %get-tuple-element.619), kind=kOutput, calls=%fused_computation.29.clone.1 | convolution fusion | flops 2417491968 | bytes 19661312 | tf_op jit(solution)/shard_map/while/body/eval_jaxpr/xzik,zkj->xij/dot_general | solution.py:21
  330.0 99.4 %while.46 = (s32[]{:T(128)}, f32[6,512,256]{2,1,0:T(8,128)S(1)}, bf16[5,6,6,6]{3,2,1,0:T(8,128)(2,1)S(1)}, bf16[5,6,512,1,256]{4,2,1,3,0:T(8,128)(2,1)}, bf16[5,...) while((s32[]{:T(128)}, f32[6,512,256]{2,1,0:T(8,128)S(1)}, ...), condition=%wide.region_2.3_spmd.clone, body=%wide.region_1.2_spmd.clone.sunk | while | flops 2474115072 | bytes 33829468 | solution.py:25
  331.5 8.8 %fusion.54 = bf16[6,6,512,256]{3,1,2,0:T(8,128)(2,1)} fusion(bf16[6,512,256,1]{2,1,0,3:T(8,128)(2,1)S(1)} %dynamic-slice_bitcast_fusion.9, bf16[5,6,6,6]{3,2,1,0:T(8,128)(2,1)S(1)} %get-tuple-element.670, s32[]{:T(128)} %get-tuple-element.661), kind=kOutput, calls=%fused_computation.6.clone.1 | convolution fusion | flops 56623104 | bytes 11022340 | tf_op jit(solution)/shard_map/while/body/eval_jaxpr/xyz,yiqn->xziqn/dot_general | solution.py:15
  340.3 9.6 %bitcast_add_fusion.6 = f32[6,512,256]{2,1,0:T(8,128)S(1)} fusion(f32[6,512,256]{2,1,0:T(8,128)S(1)} %get-tuple-element.662, bf16[6,6,512,256]{3,1,2,0:T(8,128)(2,1)} %fusion.54, pred[]{:T(512)S(6)} %compare.13, bf16[5,6,1,256,256]{4,3,1,2,0:T(8,128)(2,1)} %get-tuple-element.672, s32[]{:T(128)} %get-tuple-element.661), kind=kOutput, calls=%fused_computation.5.clone.1 | convolution fusion | flops 2417491968 | bytes 19661312 | tf_op jit(solution)/shard_map/while/body/eval_jaxpr/xzik,zkj->xij/dot_general | solution.py:21
  351.4 8.8 %fusion.54 = bf16[6,6,512,256]{3,1,2,0:T(8,128)(2,1)} fusion(bf16[6,512,256,1]{2,1,0,3:T(8,128)(2,1)S(1)} %dynamic-slice_bitcast_fusion.9, bf16[5,6,6,6]{3,2,1,0:T(8,128)(2,1)S(1)} %get-tuple-element.670, s32[]{:T(128)} %get-tuple-element.661), kind=kOutput, calls=%fused_computation.6.clone.1 | convolution fusion | flops 56623104 | bytes 11022340 | tf_op jit(solution)/shard_map/while/body/eval_jaxpr/xyz,yiqn->xziqn/dot_general | solution.py:15
  360.2 9.6 %bitcast_add_fusion.6 = f32[6,512,256]{2,1,0:T(8,128)S(1)} fusion(f32[6,512,256]{2,1,0:T(8,128)S(1)} %get-tuple-element.662, bf16[6,6,512,256]{3,1,2,0:T(8,128)(2,1)} %fusion.54, pred[]{:T(512)S(6)} %compare.13, bf16[5,6,1,256,256]{4,3,1,2,0:T(8,128)(2,1)} %get-tuple-element.672, s32[]{:T(128)} %get-tuple-element.661), kind=kOutput, calls=%fused_computation.5.clone.1 | convolution fusion | flops 2417491968 | bytes 19661312 | tf_op jit(solution)/shard_map/while/body/eval_jaxpr/xzik,zkj->xij/dot_general | solution.py:21
  371.3 8.8 %fusion.54 = bf16[6,6,512,256]{3,1,2,0:T(8,128)(2,1)} fusion(bf16[6,512,256,1]{2,1,0,3:T(8,128)(2,1)S(1)} %dynamic-slice_bitcast_fusion.9, bf16[5,6,6,6]{3,2,1,0:T(8,128)(2,1)S(1)} %get-tuple-element.670, s32[]{:T(128)} %get-tuple-element.661), kind=kOutput, calls=%fused_computation.6.clone.1 | convolution fusion | flops 56623104 | bytes 11022340 | tf_op jit(solution)/shard_map/while/body/eval_jaxpr/xyz,yiqn->xziqn/dot_general | solution.py:15
  380.1 9.6 %bitcast_add_fusion.6 = f32[6,512,256]{2,1,0:T(8,128)S(1)} fusion(f32[6,512,256]{2,1,0:T(8,128)S(1)} %get-tuple-element.662, bf16[6,6,512,256]{3,1,2,0:T(8,128)(2,1)} %fusion.54, pred[]{:T(512)S(6)} %compare.13, bf16[5,6,1,256,256]{4,3,1,2,0:T(8,128)(2,1)} %get-tuple-element.672, s32[]{:T(128)} %get-tuple-element.661), kind=kOutput, calls=%fused_computation.5.clone.1 | convolution fusion | flops 2417491968 | bytes 19661312 | tf_op jit(solution)/shard_map/while/body/eval_jaxpr/xzik,zkj->xij/dot_general | solution.py:21
  391.2 8.8 %fusion.54 = bf16[6,6,512,256]{3,1,2,0:T(8,128)(2,1)} fusion(bf16[6,512,256,1]{2,1,0,3:T(8,128)(2,1)S(1)} %dynamic-slice_bitcast_fusion.9, bf16[5,6,6,6]{3,2,1,0:T(8,128)(2,1)S(1)} %get-tuple-element.670, s32[]{:T(128)} %get-tuple-element.661), kind=kOutput, calls=%fused_computation.6.clone.1 | convolution fusion | flops 56623104 | bytes 11022340 | tf_op jit(solution)/shard_map/while/body/eval_jaxpr/xyz,yiqn->xziqn/dot_general | solution.py:15
  400.0 9.6 %bitcast_add_fusion.6 = f32[6,512,256]{2,1,0:T(8,128)S(1)} fusion(f32[6,512,256]{2,1,0:T(8,128)S(1)} %get-tuple-element.662, bf16[6,6,512,256]{3,1,2,0:T(8,128)(2,1)} %fusion.54, pred[]{:T(512)S(6)} %compare.13, bf16[5,6,1,256,256]{4,3,1,2,0:T(8,128)(2,1)} %get-tuple-element.672, s32[]{:T(128)} %get-tuple-element.661), kind=kOutput, calls=%fused_computation.5.clone.1 | convolution fusion | flops 2417491968 | bytes 19661312 | tf_op jit(solution)/shard_map/while/body/eval_jaxpr/xzik,zkj->xij/dot_general | solution.py:21
  419.9 9.6 %bitcast_add_fusion.6 = f32[6,512,256]{2,1,0:T(8,128)S(1)} fusion(f32[6,512,256]{2,1,0:T(8,128)S(1)} %get-tuple-element.662, bf16[6,6,512,256]{3,1,2,0:T(8,128)(2,1)} %fusion.54, pred[]{:T(512)S(6)} %compare.13, bf16[5,6,1,256,256]{4,3,1,2,0:T(8,128)(2,1)} %get-tuple-element.672, s32[]{:T(128)} %get-tuple-element.661), kind=kOutput, calls=%fused_computation.5.clone.1 | convolution fusion | flops 2417491968 | bytes 19661312 | tf_op jit(solution)/shard_map/while/body/eval_jaxpr/xzik,zkj->xij/dot_general | solution.py:21
  450.6 147.9 %reduce-scatter.2.cloned.1.call-done = f32[3,6,128,256]{3,2,1,0:T(8,128)} async-done(((f32[3,6,512,256]{3,2,1,0:T(8,128)}), f32[3,6,128,256]{3,2,1,0:T(8,128)}) %reduce-scatter.2.cloned.1.call-update) | async-done | bytes 2359312 | tf_op jit(solution)/shard_map/reduce_scatter | solution.py:53
  601.7 41.0 %pmax.7 = f32[3]{0:T(128)S(1)} all-reduce(f32[3]{0:T(128)S(1)} %get-tuple-element.429), channel_id=1, replica_groups=mesh['row'=2,'col'=4,'layer'=4] {'row','col','layer'}, use_global_device_ids=true, to_apply=%region_9.10 | all-reduce | flops 3 | bytes 24 | tf_op jit(solution)/shard_map/pmax | solution.py:73
  (89 shorter events, 117.8 us)
Async XLA Ops:
  7.2 21.7 %all-gather.19.cloned.1.call-start = ((), (), s32[]{:S(2)}) async-start(), calls=%async_computation.5 | async-start | bytes 5898240 | tf_op jit(solution)/shard_map/all_gather | solution.py:50
  12.7 102.4 %all-gather.17.cloned.1.call-start = ((), (), s32[]{:S(2)}) async-start(), calls=%async_computation.4 | async-start | bytes 9830400 | tf_op jit(solution)/shard_map/all_gather | solution.py:45
  18.3 205.4 %all-gather.23.cloned.1.call-start = ((), (), s32[]{:S(2)}) async-start(), calls=%async_computation.7 | async-start | bytes 5898240 | tf_op jit(solution)/shard_map/all_gather | solution.py:50
  19.0 1.9 copy-start.4
  19.0 1.9 copy-start.5
  19.1 2.6 copy-start
  19.1 204.6 %all-gather.21.cloned.1.call-start = ((), (), s32[]{:S(2)}) async-start(), calls=%async_computation.6 | async-start | bytes 9830400 | tf_op jit(solution)/shard_map/all_gather | solution.py:45
  19.6 310.4 %all-gather.15.cloned.1.call-start = ((), (), s32[]{:S(2)}) async-start(), calls=%async_computation.3 | async-start | bytes 5898240 | tf_op jit(solution)/shard_map/all_gather | solution.py:50
  20.2 309.8 %all-gather.13.cloned.1.call-start = ((), (), s32[]{:S(2)}) async-start(), calls=%async_computation.2 | async-start | bytes 9830400 | tf_op jit(solution)/shard_map/all_gather | solution.py:45
  20.8 577.6 %reduce-scatter.2.cloned.1.call-start = ((), (), s32[]{:S(2)}) async-start(), calls=%async_computation.1 | async-start | bytes 11796480 | tf_op jit(solution)/shard_map/reduce_scatter | solution.py:53
  21.0 0.6 copy-start.2
  436.8 0.7 copy-start.1
  436.8 161.6 %copy-start.3 = (f32[3]{0:T(128)S(1)}, f32[3]{0:T(128)}, u32[]{:S(2)}) copy-start(f32[3]{0:T(128)} %copy-done.2) | copy-start | bytes 40
  642.7 1.8 copy-start.6
Sparse Core Ops, SparseCore 0:
  12.8 15.9 all-gather.18
  30.7 84.4 all-gather.16
  116.7 13.2 all-gather.22
  131.7 84.4 all-gather.20
  217.5 13.2 all-gather.14
  233.1 84.4 all-gather.12
  437.0 161.4 reduce-scatter.1
where the time goes:
time: 652 us; the launch traced here: 651 us
  matrix products  294 us (45%)
  waiting for transfers between devices  243 us (37%)
  local copies, waits for them, and re-layouts  47.5 us (7%)
  blocking collectives  41 us (6%)
  between operations  14.9 us (2%)
  other arithmetic  9.5 us (1%)
    dot_general x15, matrix products, one_split(): jnp.einsum('xzik,zkj->xij', mixed_part, right_part, preferred_element_typ...  159 us
    reduce_scatter x1, waiting for transfers between devices, local(): summed = lax.psum_scatter(summed, 'layer', scatter_dimension=2, tiled=True)  148 us
    dot_general x15, matrix products, one_split(): jnp.einsum('xyz,yiqn->xziqn', mixing_now, left_part, preferred_element_ty...  132 us
    all_gather x3, waiting for transfers between devices, local(): lax.all_gather(left_mant[block_id], 'col', axis=2, tiled=True)  86.3 us
    pmax x1, blocking collectives, local(): lax.pmax(jnp.max(inside, axis=(1, 2, 3)), ('row', 'col', 'layer'))  41 us
    another operation x15, local copies, waits for them, and re-layouts  23.2 us
  transfers between devices with their start and end apart: 7, of which 3 were waited for; matrix products, arithmetic and copies ran while one was open for 36% of the time, Pallas kernels for 0%

commit v1 on v0

--- a/solution.py
+++ b/solution.py
@@ -3,7 +3,13 @@
 import jax
 import jax.numpy as jnp
 from jax import lax
+from jax.experimental import pallas as pl
+from jax.experimental.pallas import tpu as pltpu
 from jax.sharding import PartitionSpec as P
+
+
+TILE = 32
+VMEM_BYTES = 63 * 1024 * 1024
 
 
 def add_pieces(left_full, mix_block, running, arrived, anchor):
@@ -74,6 +80,375 @@
     return (inside - peak_value[:, None, None, None], peak_value)
 
 
+MESH = pl.DeviceIdType.MESH
+LAG = 2
+
+
+def flip(first, second):
+    low = lax.rem(first + second, 2)
+    high = lax.rem(first // 2 + second // 2, 2)
+    return low + 2 * high
+
+
+def fused(
+    sizes, left_ref, right_ref, spread_ref, chosen_ref, codes_ref, out_ref, peak_ref,
+    lefts, rights, sums, landed, landed_top, mixed, expand, peaks,
+    own_sem, right_sem, right_send, right_recv, side_send, side_recv, pass_send, pass_recv,
+    sum_send, sum_recv, top_recv, peak_send, peak_recv, out_sem,
+):
+    count_out, count_split, channels, rows, width, depth, cols, tile = sizes
+    row, col, layer = lax.axis_index("row"), lax.axis_index("col"), lax.axis_index("layer")
+    other = 1 - row
+    sides = (flip(col, 1), flip(col, 2))
+    half = channels // 2
+    total = count_out * 4
+
+    barrier = pltpu.get_barrier_semaphore()
+    greeted = [{"row": other}, {"col": sides[0]}, {"col": sides[1]}]
+    greeted += [{"layer": lax.rem(layer + step, 4)} for step in (1, 2, 3)]
+    for device in greeted:
+        pl.semaphore_signal(barrier, inc=1, device_id=device, device_id_type=MESH)
+    pl.semaphore_wait(barrier, len(greeted))
+
+    def own_copy(b):
+        return pltpu.make_async_copy(left_ref.at[b], lefts.at[b, 0], own_sem.at[b])
+
+    def right_copy(b):
+        place = rights.at[b, :, :, pl.ds(pl.multiple_of(row * depth, depth), depth)]
+        return pltpu.make_async_copy(right_ref.at[b], place, right_sem.at[b])
+
+    def right_share(b):
+        place = rights.at[b, :, :, pl.ds(pl.multiple_of(row * depth, depth), depth)]
+        return pltpu.make_async_remote_copy(
+            right_ref.at[b], place, right_send.at[b], right_recv.at[b],
+            device_id={"row": other}, device_id_type=MESH,
+        )
+
+    def side_share(b, side, part):
+        return pltpu.make_async_remote_copy(
+            left_ref.at[b, :, pl.ds(part * half, half)],
+            lefts.at[b, side + 1, :, pl.ds(part * half, half)],
+            side_send.at[b, side, part], side_recv.at[b, side, part],
+            device_id={"col": sides[side]}, device_id_type=MESH,
+        )
+
+    def pass_on(b, side):
+        return pltpu.make_async_remote_copy(
+            lefts.at[b, side + 1, :, pl.ds(side * half, half)],
+            lefts.at[b, 3, :, pl.ds(side * half, half)],
+            pass_send.at[b, side], pass_recv.at[b, side],
+            device_id={"col": sides[1 - side]}, device_id_type=MESH,
+        )
+
+    def start_block(b):
+        right_share(b).start()
+        for part in (0, 1):
+            for side in (0, 1):
+                side_share(b, side, part if side == 0 else 1 - part).start()
+        own_copy(b).start()
+        right_copy(b).start()
+
+    def sum_share(b, slot, up):
+        return pltpu.make_async_remote_copy(
+            sums.at[b, slot], landed.at[b, slot], sum_send.at[b, slot], sum_recv.at[b, slot],
+            device_id={"layer": lax.rem(layer + (1 if up else 3), 4)}, device_id_type=MESH,
+        )
+
+    def sum_share_top(b, slot):
+        return pltpu.make_async_remote_copy(
+            sums.at[b, slot], landed_top.at[b], sum_send.at[b, slot], top_recv.at[b],
+            device_id={"layer": lax.rem(layer + 3, 4)}, device_id_type=MESH,
+        )
+
+    def add_landed(b, slot, source):
+        def add(x, carry):
+            sums[b, slot, x] = sums[b, slot, x] + source[x]
+            return carry
+        lax.fori_loop(0, channels, add, 0)
+
+    def relay(index, hop):
+        b, slot = index // 4, lax.rem(index, 4)
+        owner = flip(col, slot)
+
+        def arrive():
+            if hop:
+                sum_share(b, slot, True).wait_recv()
+                add_landed(b, slot, landed.at[b, slot])
+
+        @pl.when((owner > layer) & (layer == hop))
+        def _():
+            arrive()
+            sum_share(b, slot, True).start()
+
+        @pl.when((owner < layer) & (3 - layer == hop))
+        def _():
+            arrive()
+
+            @pl.when(owner == layer - 1)
+            def _():
+                sum_share_top(b, slot).start()
+
+            @pl.when(owner < layer - 1)
+            def _():
+                sum_share(b, slot, False).start()
+
+    same = (
+        lax.broadcasted_iota(jnp.int32, (tile, channels * tile), 0)
+        == lax.rem(lax.broadcasted_iota(jnp.int32, (tile, channels * tile), 1), tile)
+    )
+
+    def compute(b, slot):
+        def one_split(s, carry):
+            for zx in range(channels * channels):
+                line = spread_ref[b * count_split + s, zx:zx + 1, :]
+                expand[zx * tile:(zx + 1) * tile, :] = jnp.where(same, line, 0.0).astype(jnp.bfloat16)
+
+            def one_tile(i, carry):
+                start = pl.multiple_of(i * tile, tile)
+                piece = lefts[b, slot, s, :, pl.ds(start, tile), :].reshape(channels * tile, width)
+                whole = jnp.dot(expand[...], piece, preferred_element_type=jnp.float32)
+                whole = whole.astype(jnp.bfloat16)
+                for z in range(channels):
+                    for x in range(channels):
+                        at = (z * channels + x) * tile
+                        mixed[pl.ds(x * rows + start, tile), z * width:(z + 1) * width] = whole[at:at + tile]
+                return carry
+
+            lax.fori_loop(0, rows // tile, one_tile, 0)
+            right = rights[b, s].reshape(channels * width, cols)
+            for x in range(channels):
+                term = jnp.dot(
+                    mixed[x * rows:(x + 1) * rows, :], right, preferred_element_type=jnp.float32
+                )
+                before = jnp.where(s == 0, 0.0, sums[b, slot, x])
+                sums[b, slot, x] = before + term
+            return carry
+
+        lax.fori_loop(0, count_split, one_split, 0)
+
+    peaks[0] = jnp.full_like(peaks[0], -jnp.inf)
+
+    def finish(b):
+        slot = flip(col, layer)
+
+        @pl.when(layer > 0)
+        def _():
+            sum_share(b, slot, True).wait_recv()
+            add_landed(b, slot, landed.at[b, slot])
+
+        @pl.when(layer < 3)
+        def _():
+            sum_share_top(b, slot).wait_recv()
+            add_landed(b, slot, landed_top.at[b])
+
+        def one_channel(x, best):
+            code = codes_ref[b]
+            pairing = chosen_ref[b, x, 3:4, :]
+            for u in (2, 1, 0):
+                pairing = jnp.where(code == u, chosen_ref[b, x, u:u + 1, :], pairing)
+            value = jnp.log(sums[b, slot, x]) + pairing
+            sums[b, slot, x] = value
+            return jnp.maximum(best, jnp.max(value, axis=0, keepdims=True))
+
+        best = lax.fori_loop(0, channels, one_channel, jnp.full((1, cols), -jnp.inf, jnp.float32))
+        best = jnp.max(best, axis=1, keepdims=True)
+        at = lax.broadcasted_iota(jnp.int32, peaks.shape[1:], 0)
+        peaks[0] = jnp.where(at == b, best, peaks[0])
+
+    start_block(0)
+
+    def step(t, carry):
+        b, slot = t // 4, lax.rem(t, 4)
+
+        @pl.when((slot == 0) & (t >= 8))
+        def _():
+            finish(b - 2)
+
+        @pl.when(t < total)
+        def _():
+            @pl.when(slot == 0)
+            def _():
+                own_copy(b).wait()
+                right_copy(b).wait()
+                right_share(b).wait_recv()
+
+            @pl.when(slot == 1)
+            def _():
+                side_share(b, 0, 0).wait_recv()
+                pass_on(b, 0).start()
+                side_share(b, 1, 1).wait_recv()
+                pass_on(b, 1).start()
+
+                @pl.when(b < count_out - 1)
+                def _():
+                    start_block(b + 1)
+
+                side_share(b, 0, 1).wait_recv()
+
+            @pl.when(slot == 2)
+            def _():
+                side_share(b, 1, 0).wait_recv()
+
+            @pl.when(slot == 3)
+            def _():
+                pass_on(b, 0).wait_recv()
+                pass_on(b, 1).wait_recv()
+
+            compute(b, slot)
+            relay(t, 0)
+
+        for hop in (1, 2):
+            @pl.when((t >= hop * LAG) & (t - hop * LAG < total))
+            def _(hop=hop):
+                relay(t - hop * LAG, hop)
+        return carry
+
+    lax.fori_loop(0, total + 4, step, 0)
+    finish(count_out - 1)
+
+    def swap(number, device):
+        copy = pltpu.make_async_remote_copy(
+            peaks.at[number], peaks.at[4 + number], peak_send.at[number], peak_recv.at[number],
+            device_id=device, device_id_type=MESH,
+        )
+        copy.start()
+        copy.wait()
+        peaks[number + 1] = jnp.maximum(peaks[number], peaks[4 + number])
+
+    swap(0, {"row": other})
+    swap(1, {"col": sides[0]})
+    swap(2, {"col": sides[1]})
+    copies = []
+    for distance in (1, 2, 3):
+        copy = pltpu.make_async_remote_copy(
+            peaks.at[3], peaks.at[6 + distance], peak_send.at[2 + distance], peak_recv.at[2 + distance],
+            device_id={"layer": lax.rem(layer + distance, 4)}, device_id_type=MESH,
+        )
+        copy.start()
+        copies.append(copy)
+    top = peaks[3]
+    for distance, copy in zip((1, 2, 3), copies):
+        copy.wait()
+        top = jnp.maximum(top, peaks[6 + distance])
+    peak_ref[...] = top
+
+    slot = flip(col, layer)
+    outs = []
+    for b in range(count_out):
+        level = top[b:b + 1, 0:1]
+
+        def lower(x, carry):
+            sums[b, slot, x] = sums[b, slot, x] - level
+            return carry
+
+        lax.fori_loop(0, channels, lower, 0)
+        copy = pltpu.make_async_copy(sums.at[b, slot], out_ref.at[b], out_sem.at[b])
+        copy.start()
+        outs.append(copy)
+
+    def settle(b, carry):
+        right_share(b).wait_send()
+        for side in (0, 1):
+            pass_on(b, side).wait_send()
+            for part in (0, 1):
+                side_share(b, side, part).wait_send()
+        for slot in range(4):
+            @pl.when(flip(col, slot) != layer)
+            def _(slot=slot):
+                sum_share(b, slot, True).wait_send()
+        return carry
+
+    lax.fori_loop(0, count_out, settle, 0)
+    for copy in outs:
+        copy.wait()
+
+
+def local_fused(
+    left_mant, right_mant, left_scale, right_scale, rule_probs, pair_logp, nucleotides, first_block
+):
+    total_scale = left_scale + right_scale
+    highest = jnp.max(total_scale, axis=1)
+    weight = jnp.exp(total_scale - highest[:, None])
+    mixing = (rule_probs[None, None] * weight[:, :, None, None, None]).astype(jnp.bfloat16)
+    count_out, count_split, channels, rows, _, width = left_mant.shape
+    depth, cols = right_mant.shape[4:]
+    tile = TILE
+    row, col, layer = lax.axis_index("row"), lax.axis_index("col"), lax.axis_index("layer")
+    block_len = cols * lax.axis_size("col")
+
+    spread = mixing.astype(jnp.float32).transpose(0, 1, 4, 2, 3)
+    spread = spread.reshape(count_out * count_split, channels * channels, channels, 1)
+    spread = jnp.broadcast_to(spread, spread.shape[:3] + (tile,))
+    spread = spread.reshape(count_out * count_split, channels * channels, channels * tile)
+
+    by_block = nucleotides.reshape(-1, block_len)
+    row_anchor = (row * lax.axis_size("layer") + layer) * rows
+    row_codes = lax.dynamic_slice(by_block, (first_block[0], row_anchor), (count_out, rows))
+    col_codes = lax.dynamic_slice(
+        by_block, (first_block[0] + count_split + 1, col * cols), (count_out, cols)
+    )
+    codes = jnp.broadcast_to(row_codes[:, :, None], (count_out, rows, cols))
+    seen = col_codes[:, None, None, :]
+    pairs = pair_logp[None, :, :, :, None]
+    chosen = pairs[:, :, :, 3]
+    for v in (2, 1, 0):
+        chosen = jnp.where(seen == v, pairs[:, :, :, v], chosen)
+
+    sizes = (count_out, count_split, channels, rows, width, depth, cols, tile)
+    f32, bf16 = jnp.float32, jnp.bfloat16
+    in_vmem = pl.BlockSpec(memory_space=pltpu.VMEM)
+    anywhere = pl.BlockSpec(memory_space=pl.ANY)
+    dma = pltpu.SemaphoreType.DMA
+    flops = 2 * count_out * count_split * channels * channels * 4 * rows * width * cols
+    values, peaks = pl.pallas_call(
+        partial(fused, sizes),
+        out_shape=(
+            jax.ShapeDtypeStruct((count_out, channels, rows, cols), f32),
+            jax.ShapeDtypeStruct((8, 128), f32),
+        ),
+        in_specs=[anywhere, anywhere, in_vmem, in_vmem, in_vmem],
+        out_specs=(anywhere, in_vmem),
+        scratch_shapes=[
+            pltpu.VMEM((count_out, 4, count_split, channels, rows, width), bf16),
+            pltpu.VMEM((count_out, count_split, channels, width, cols), bf16),
+            pltpu.VMEM((count_out, 4, channels, rows, cols), f32),
+            pltpu.VMEM((count_out, 4, channels, rows, cols), f32),
+            pltpu.VMEM((count_out, channels, rows, cols), f32),
+            pltpu.VMEM((channels * rows, channels * width), bf16),
+            pltpu.VMEM((channels * channels * tile, channels * tile), bf16),
+            pltpu.VMEM((10, 8, 128), f32),
+            dma((count_out,)), dma((count_out,)), dma((count_out,)), dma((count_out,)),
+            dma((count_out, 2, 2)), dma((count_out, 2, 2)),
+            dma((count_out, 2)), dma((count_out, 2)),
+            dma((count_out, 4)), dma((count_out, 4)), dma((count_out,)),
+            dma((6,)), dma((6,)), dma((count_out,)),
+        ],
+        compiler_params=pltpu.CompilerParams(
+            collective_id=0, has_side_effects=True, vmem_limit_bytes=VMEM_BYTES
+        ),
+        cost_estimate=pl.CostEstimate(
+            flops=flops, bytes_accessed=left_mant.size * 8, transcendentals=count_out * channels * rows * cols
+        ),
+    )(
+        left_mant.reshape(count_out, count_split, channels, rows, width),
+        right_mant.reshape(count_out, count_split, channels, depth, cols),
+        spread, chosen, codes,
+    )
+    return values, peaks[:count_out, 0] + highest
+
+
+def fits_fused(shape, args):
+    left, right = args[0].shape, args[1].shape
+    rows, depth, cols = left[3] // (shape["row"] * shape["col"]), right[4] // shape["row"], right[5] // shape["col"]
+    return (
+        shape["row"] == 2 and shape["col"] == 4 and shape["layer"] == 4
+        and left[4] == 4 and right[3] == 4 and left[0] <= 3 and left[2] % 2 == 0
+        and rows * 8 == left[3] and rows % TILE == 0 and depth % 16 == 0 and left[5] == 2 * depth
+        and left[5] % 128 == 0 and cols % 128 == 0 and left[3] == right[5]
+        and left[0] * left[1] * left[2] * rows * left[5] <= VMEM_BYTES // 20
+    )
+
+
 def solution(mesh):
     in_specs = (
         P(None, None, None, ("row", "col"), "layer", None),
@@ -86,4 +461,11 @@
         P(),
     )
     out_specs = (P(None, None, ("row", "layer"), "col"), P())
-    return jax.shard_map(local, mesh=mesh, in_specs=in_specs, out_specs=out_specs, check_vma=False)
+
+    def whole(*args):
+        body = local_fused if fits_fused(mesh.shape, args) else local
+        return jax.shard_map(
+            body, mesh=mesh, in_specs=in_specs, out_specs=out_specs, check_vma=False
+        )(*args)
+
+    return whole

time: 652 us -> 296 us (0.45)
  matrix products: 294 us -> 0 us
  Pallas kernels: 0 us -> 281 us
  waiting for transfers between devices: 243 us -> 0 us
  blocking collectives: 41 us -> 0 us
  local copies, waits for them, and re-layouts: 47.5 us -> 10.8 us
  between operations: 14.9 us -> 1.34 us
  other arithmetic: 9.5 us -> 2.29 us
    dot_general x32 -> x0, matrix products: 294 us -> none  [the longest x15 159 us: one_split(): jnp.einsum('xzik,zkj->xij', mixed_part, right_part, preferred_element_typ...]
    pallas_call x0 -> x1, Pallas kernels: none -> 281 us  [local_fused(): pl.pallas_call(partial(fused, sizes), out_shape=(jax.ShapeDtypeStruct((co...]
    reduce_scatter x1 -> x0, waiting for transfers between devices: 148 us -> none  [local(): summed = lax.psum_scatter(summed, 'layer', scatter_dimension=2, tiled=True)]
    all_gather x6 -> x0, waiting for transfers between devices: 93.3 us -> none  [the longest x3 86.3 us: local(): lax.all_gather(left_mant[block_id], 'col', axis=2, tiled=True)]
    pmax x1 -> x0, blocking collectives: 41 us -> none  [local(): lax.pmax(jnp.max(inside, axis=(1, 2, 3)), ('row', 'col', 'layer'))]
    another operation x15 -> x0, local copies, waits for them, and re-layouts: 23.2 us -> none
    gather x18 -> x0, local copies, waits for them, and re-layouts: 12.5 us -> none
    slice x2, local copies, waits for them, and re-layouts: 11 us -> 1.65 us  [the longest x1 0.86 us: local_fused(): chosen = jnp.where(seen == v, pairs[:, :, :, v], chosen)]
  transfers between devices with their start and end apart: 7 -> 0, of which waited for: 3 -> 0; matrix products, arithmetic and copies ran while one was open for 36% -> 0% of each run, Pallas kernels for 0% -> 0%
where the time goes in v1:
time: 296 us
  Pallas kernels  281 us (95%)
  local copies, waits for them, and re-layouts  10.8 us (4%)
    pallas_call x1, Pallas kernels, local_fused(): pl.pallas_call(partial(fused, sizes), out_shape=(jax.ShapeDtypeStruct((co...  281 us

profile of v1, /device:TPU:0, one launch (start us, length us, event | category | flops | bytes accessed | tf_op | source)
XLA Modules:
  0.0 295.7 jit_solution(15389482177134327921)
XLA Ops:
  1.3 0.8 fusion.1
  2.1 0.1 subtract_exponential_fusion
  2.2 0.1 mul.36
  2.3 0.9 fusion.2
  3.1 0.1 copy.26
  3.2 0.1 copy.23
  3.3 0.1 copy.25
  3.4 0.1 copy.24
  3.5 0.9 copy.21
  4.4 0.1 mul.34
  4.4 0.1 fusion
  4.5 0.2 copy.22
  4.8 1.0 reshape.40
  5.8 0.1 dynamic_slice.7
  5.8 0.1 dynamic-slice_compare_fusion.2
  5.9 0.7 select_select_fusion.chosen_ref
  6.7 0.9 broadcast_in_dim.89.codes_ref
  7.5 0.6 broadcast_in_dim.76
  8.2 0.5 reshape.39
  8.7 1.1 copy.27.spread_ref
  9.8 281.3 %shard_map.95 = (f32[3,6,128,256]{3,2,1,0:T(8,128)}, f32[8,128]{1,0:T(8,128)}) custom-call(bf16[3,5,6,128,256]{4,3,2,1,0:T(8,128)(2,1)} %bitcast.24, bf16[3,5,6,128,256]{4,3,2,1,0:T(8,128)(2,1)} %bitcast.25, f32[15,36,192]{2,1,0:T(8,128)} %copy.27.spread_ref, f32[3,6,4,256]{3,2,1,0:T(4,128)} %select_select_fusion.chosen_ref, ...), custom_call_target="tpu_custom_call" | custom-call | flops 36238786560 | bytes 23592960 | tf_op jit(solution)/shard_map/pallas_call | solution.py:403
  291.1 0.8 slice_reduce_fusion
  291.9 0.5 add.36
  292.4 3.3 %copy.30 = f32[3,6,128,256]{3,2,1,0:T(8,128)} copy(f32[3,6,128,256]{3,2,1,0:T(8,128)} %get-tuple-element.17) | data formatting | bytes 4718592
